TPU v7x, 32 devices: a whole 2x2x4 slice. The times are simulated.
32 devices in a mesh: dp: 8 (over y, x, core), tensor: 4 (over z).
Axes of the slice: x: 2, y: 2, z: 4, core: 2. Of those that a mesh axis runs over, the one named last changes fastest.
Arguments:
- qkv: bfloat16 [4, 640, 3, 4096], P(None, 'dp', None, 'tensor'), may hold values from -6 to 6
- fir_buffer: bfloat16 [640, 3, 2, 4096], P('dp', None, None, 'tensor'), may hold values from -6 to 6
- fir_taps: float32 [3, 3, 4096], P(None, None, 'tensor'), may hold values from -3 to 3
- modal_state: float32 [640, 16, 4096], P('dp', None, 'tensor'), may hold values from -6 to 6
- poles: float32 [16, 4096], P(None, 'tensor'), may hold values from 0.5 to 0.999
- residues: float32 [16, 4096], P(None, 'tensor'), may hold values from -1.5 to 1.5
- skip: float32 [4096], P('tensor'), may hold values from -3 to 3
- out_weight: bfloat16 [4096, 4096], P('tensor')
- norm_gain: float32 [4096], P('tensor'), may hold values from 0.25 to 1.75
- finished: int32 [3, 640], P(None, 'dp'), may hold values 0 or 1
- dest_group: int32 [3, 640], P(None, 'dp'), may hold values from 0 to 7, as said below
Outputs:
- mixed: bfloat16 [4, 640, 4096], P(None, 'dp', 'tensor')
- final_state: float32 [640, 16, 4096], P('dp', None, 'tensor')
- final_lagged: bfloat16 [640, 3, 2, 4096], P('dp', None, None, 'tensor')
Inputs may be any that keep to these rules, and one draw needn't show every extreme that they name: `dest_group`: for each migration, the slots s < 16 of every group form bands of 2 slots; all rows of band b of group g go to group (g + k_b) mod 8, where k_b is the same for every group and takes each value of 0 to 7 for exactly one band. Rows in later slots stay. So each group sends exactly 2 rows to every group and the moves are a permutation of the rows.
All inputs are finite; a program needn't handle non-finite values. No bound on the sum of `finished` on one device may be relied on, other than what follows from the above.
Results may differ from a plain program's by a relative error of at most 0.0048.
Values may be sent and summed in bfloat16 or wider, within the bound.
A program may use at most 128 MiB of HBM per device.

v0:
```python
import jax
import jax.numpy as jnp
from jax import lax
from jax.sharding import PartitionSpec as P

STEPS = 4
CAP = 2


def migrate(state_now, lagged, dropped, plan_row):
    alive = (1 - dropped).astype(jnp.float32)
    state_now = state_now * alive[:, None, None]
    lagged = lagged * alive.astype(jnp.bfloat16)[:, None, None, None]
    groups = lax.axis_size("dp")
    own_group = lax.axis_index("dp")
    band_rows = groups * CAP
    group_ids = jnp.arange(groups, dtype=jnp.int32)
    band_target = plan_row[0:band_rows:CAP]
    picked = (band_target[None, :] == group_ids[:, None]).astype(jnp.int32)
    band_for = jnp.sum(picked * group_ids[None, :], axis=1)
    state_bands = state_now[:band_rows].reshape((groups, CAP) + state_now.shape[1:])
    lag_bands = lagged[:band_rows].reshape((groups, CAP) + lagged.shape[1:])
    got_state = lax.all_to_all(state_bands[band_for], "dp", split_axis=0, concat_axis=0, tiled=True)
    got_lag = lax.all_to_all(lag_bands[band_for], "dp", split_axis=0, concat_axis=0, tiled=True)
    band_shift = (band_target - own_group + groups) % groups
    source = (own_group - band_shift + groups) % groups
    new_state = got_state[source].reshape((band_rows,) + state_now.shape[1:])
    new_lag = got_lag[source].reshape((band_rows,) + lagged.shape[1:])
    state_now = jnp.concatenate([new_state, state_now[band_rows:]], axis=0)
    lagged = jnp.concatenate([new_lag, lagged[band_rows:]], axis=0)
    return (state_now, lagged)


def per_device(
    qkv,
    fir_buffer,
    fir_taps,
    modal_state,
    poles,
    residues,
    skip,
    out_weight,
    norm_gain,
    finished,
    dest_group,
):
    state_now = modal_state
    lagged = fir_buffer
    own_cols = norm_gain.shape[0]
    results = []
    for turn_index in range(STEPS):
        incoming = qkv[turn_index]
        filtered = fir_taps[None, :, 0, :] * incoming.astype(jnp.float32)
        filtered = filtered + fir_taps[None, :, 1, :] * lagged[:, :, 0, :].astype(jnp.float32)
        filtered = filtered + fir_taps[None, :, 2, :] * lagged[:, :, 1, :].astype(jnp.float32)
        lagged = jnp.stack([incoming, lagged[:, :, 0, :]], axis=2)
        product = filtered[:, 1] * filtered[:, 2]
        state_now = poles[None] * state_now + product[:, None, :]
        modal_out = jnp.sum(residues[None] * state_now, axis=1) + skip[None] * product
        gated_out = (filtered[:, 0] * modal_out).astype(jnp.bfloat16)
        partial_out = jnp.dot(gated_out, out_weight, preferred_element_type=jnp.float32)
        summed = lax.psum(partial_out, "tensor")
        mean_square = jnp.mean(summed * summed, axis=1)
        own_part = lax.dynamic_slice_in_dim(
            summed, lax.axis_index("tensor") * own_cols, own_cols, 1
        )
        norm_scale = lax.rsqrt(mean_square + 1e-05)
        results.append((own_part * norm_scale[:, None] * norm_gain[None]).astype(jnp.bfloat16))
        if turn_index < STEPS - 1:
            state_now, lagged = migrate(
                state_now, lagged, finished[turn_index], dest_group[turn_index]
            )
    return (jnp.stack(results), state_now, lagged)


def solution(mesh):
    return jax.shard_map(
        per_device,
        mesh=mesh,
        in_specs=(
            P(None, "dp", None, "tensor"),
            P("dp", None, None, "tensor"),
            P(None, None, "tensor"),
            P("dp", None, "tensor"),
            P(None, "tensor"),
            P(None, "tensor"),
            P("tensor"),
            P("tensor", None),
            P("tensor"),
            P(None, "dp"),
            P(None, "dp"),
        ),
        out_specs=(P(None, "dp", "tensor"), P("dp", None, "tensor"), P("dp", None, None, "tensor")),
        check_vma=False,
    )
```

profile of v0, /device:TPU:0, one launch (start us, length us, event | category | flops | bytes accessed | tf_op | source)
XLA Modules:
  0.0 367.5 jit_solution(5028171482460122517)
XLA Ops:
  10.3 2.6 slice_bitcast_fusion
  18.0 5.2 %all-to-all-start = ((bf16[8,2,3,2,1024]{4,3,2,1,0:T(2,128)(2,1)}), bf16[8,2,3,2,1024]{4,3,2,1,0:T(2,128)(2,1)}, u32[]{:S(2)}, u32[]{:S(2)}) async-start(bf16[8,2,3,2,1024]{4,3,2,1,0:T(2,128)(2,1)} %gather_fusion), calls=%async_computation | async-start | bytes 393216 | tf_op jit(solution)/shard_map/all_to_all | solution.py:24
  23.5 3.1 fusion.3
  26.6 2.3 copy-done.2
  30.1 2.8 gather_fusion.2
  32.9 4.2 %all-to-all-start.1 = ((f32[8,2,16,1024]{3,2,1,0:T(8,128)}), f32[8,2,16,1024]{3,2,1,0:T(8,128)}, u32[]{:S(2)}, u32[]{:S(2)}) async-start(f32[8,2,16,1024]{3,2,1,0:T(8,128)} %gather_fusion.2), calls=%async_computation.1 | async-start | bytes 2097152 | tf_op jit(solution)/shard_map/all_to_all | solution.py:23
  37.1 2.1 slice.233
  39.3 4.7 %slice.238 = f32[64,16,1024]{2,1,0:T(8,128)} slice(f32[80,16,1024]{2,1,0:T(8,128)} %copy-done.2), slice={[16:80], [0:16], [0:1024]} | slice | bytes 8388608 | tf_op jit(solution)/shard_map/slice | solution.py:29
  52.2 2.5 gather_fusion.4
  55.5 4.2 %all-to-all-start.2 = ((bf16[8,2,3,2,1024]{4,1,2,3,0:T(2,128)(2,1)}), bf16[8,2,3,2,1024]{4,1,2,3,0:T(2,128)(2,1)}, u32[]{:S(2)}, u32[]{:S(2)}) async-start(bf16[8,2,3,2,1024]{4,1,2,3,0:T(2,128)(2,1)} %gather_fusion.4), calls=%async_computation.2 | async-start | bytes 393216 | tf_op jit(solution)/shard_map/all_to_all | solution.py:24
  61.5 2.9 fusion.5
  64.4 2.3 copy-done
  67.8 2.9 gather_fusion.6
  70.7 4.2 %all-to-all-start.3 = ((f32[8,2,16,1024]{3,2,1,0:T(8,128)}), f32[8,2,16,1024]{3,2,1,0:T(8,128)}, u32[]{:S(2)}, u32[]{:S(2)}) async-start(f32[8,2,16,1024]{3,2,1,0:T(8,128)} %gather_fusion.6), calls=%async_computation.3 | async-start | bytes 2097152 | tf_op jit(solution)/shard_map/all_to_all | solution.py:23
  77.1 2.5 gather_fusion.5
  83.1 2.4 fusion.8
  89.6 4.8 %slice.247 = f32[64,16,1024]{2,1,0:T(8,128)} slice(f32[80,16,1024]{2,1,0:T(8,128)} %copy-done), slice={[16:80], [0:16], [0:1024]} | slice | bytes 8388608 | tf_op jit(solution)/shard_map/slice | solution.py:29
  94.4 4.2 %all-to-all-start.4 = ((bf16[8,2,3,2,1024]{4,3,2,1,0:T(2,128)(2,1)}), bf16[8,2,3,2,1024]{4,3,2,1,0:T(2,128)(2,1)S(1)}, u32[]{:S(2)}, u32[]{:S(2)}) async-start(bf16[8,2,3,2,1024]{4,3,2,1,0:T(2,128)(2,1)} %gather_fusion.8), calls=%async_computation.4 | async-start | bytes 393216 | tf_op jit(solution)/shard_map/all_to_all | solution.py:24
  100.4 2.8 fusion.4
  103.2 2.3 copy-done.1
  106.8 2.9 gather_fusion.10
  109.6 4.2 %all-to-all-start.5 = ((f32[8,2,16,1024]{3,2,1,0:T(8,128)}), f32[8,2,16,1024]{3,2,1,0:T(8,128)}, u32[]{:S(2)}, u32[]{:S(2)}) async-start(f32[8,2,16,1024]{3,2,1,0:T(8,128)} %gather_fusion.10), calls=%async_computation.5 | async-start | bytes 2097152 | tf_op jit(solution)/shard_map/all_to_all | solution.py:23
  117.3 2.4 fusion.6
  121.4 4.8 %slice.256 = f32[64,16,1024]{2,1,0:T(8,128)} slice(f32[80,16,1024]{2,1,0:T(8,128)} %copy-done.1), slice={[16:80], [0:16], [0:1024]} | slice | bytes 8388608 | tf_op jit(solution)/shard_map/slice | solution.py:29
  126.2 3.2 all-to-all-done.5
  129.3 2.9 gather_fusion.11
  132.2 12.4 %multiply_reduce_fusion.3 = (f32[80,1024]{1,0:T(8,128)S(1)}, f32[80,1024]{1,0:T(8,128)S(1)}, f32[80,1024]{1,0:T(8,128)S(1)}, f32[80,1024]{1,0:T(8,128)S(1)}, f32[80,16,1024]{2,1,0:T(8,128)}) fusion(f32[80,16,1024]{2,1,0:T(8,128)} %param.14, f32[80,1024]{1,0:T(8,128)S(1)} %fusion.29, f32[16,1024]{1,0:T(8,128)S(1)} %copy-done.19, ...), kind=kLoop, calls=%fused_computation.21 | loop fusion | flops 24576000 | bytes 28966912 | tf_op jit(solution)/shard_map/reduce_sum | solution.py:59
  144.7 6.2 %fusion.42 = f32[80,4096]{1,0:T(8,128)} fusion(bf16[1024,4096]{1,0:T(8,128)(2,1)} %param.18, f32[80,3,1024]{2,0,1:T(8,128)S(1)} %copy-done.9, f32[80,1024]{1,0:T(8,128)S(1)} %get-tuple-element.15, f32[80,1024]{1,0:T(8,128)S(1)} %copy-done.12, f32[1024]{0:T(1024)S(1)} %copy-done.20), kind=kOutput, calls=%fused_computation.106 | convolution fusion | flops 671416320 | bytes 10686464 | tf_op jit(solution)/shard_map/dot_general | solution.py:61
  150.9 6.2 %fusion.40 = f32[80,4096]{1,0:T(8,128)} fusion(bf16[1024,4096]{1,0:T(8,128)(2,1)} %param.18, f32[80,3,1024]{2,0,1:T(8,128)S(1)} %copy-done.7, f32[80,1024]{1,0:T(8,128)S(1)} %get-tuple-element.14, f32[80,1024]{1,0:T(8,128)S(1)} %fusion.23, f32[1024]{0:T(1024)S(1)} %copy-done.20), kind=kOutput, calls=%fused_computation.105 | convolution fusion | flops 671416320 | bytes 10686464 | tf_op jit(solution)/shard_map/dot_general | solution.py:61
  157.1 2.6 fusion.36
  159.7 2.6 fusion.38
  165.6 186.6 %all-reduce.3.cloned.1.call-done = (f32[80,4096]{1,0:T(8,128)}, f32[80,4096]{1,0:T(8,128)}, f32[80,4096]{1,0:T(8,128)}, f32[80,4096]{1,0:T(8,128)}) async-done(((f32[80,4096]{1,0:T(8,128)}, f32[80,4096]{1,0:T(8,128)}, f32[80,4096]{1,0:T(8,128)}, f32[80,4096]{1,0:T(8,128)}), (f32[80,4096]{1,0:T(8,128)}, f32[80,4096]{1,0:T(8,128)}, f32[80,4096]{1,0:T(8,128)}, ...) | async-done | bytes 5242896 | tf_op jit(solution)/shard_map/psum | solution.py:62
  (120 shorter events, 50.8 us)
Async XLA Ops:
  7.2 7.2 %copy-start.3 = (bf16[4,80,3,1024]{3,1,2,0:T(8,128)(2,1)S(1)}, bf16[4,80,3,1024]{3,1,2,0:T(8,128)(2,1)}, u32[]{:S(2)}) copy-start(bf16[4,80,3,1024]{3,1,2,0:T(8,128)(2,1)} %param.11) | copy-start | bytes 5898244
  7.2 5.7 %copy-start.16 = (bf16[80,3,2,1024]{3,2,1,0:T(2,128)(2,1)S(1)}, bf16[80,3,2,1024]{3,2,1,0:T(2,128)(2,1)}, u32[]{:S(2)}) copy-start(bf16[80,3,2,1024]{3,2,1,0:T(2,128)(2,1)} %param.12) | copy-start | bytes 2949124
  14.3 9.2 %copy-start.19 = (f32[16,1024]{1,0:T(8,128)S(1)}, f32[16,1024]{1,0:T(8,128)}, u32[]{:S(2)}) copy-start(f32[16,1024]{1,0:T(8,128)} %param.15) | copy-start | bytes 196612
  14.9 11.7 %copy-start.10 = (f32[80,3,1024]{2,0,1:T(8,128)}, f32[80,3,1024]{2,0,1:T(8,128)S(1)}, u32[]{:S(2)}) copy-start(f32[80,3,1024]{2,0,1:T(8,128)S(1)} %get-tuple-element.25) | copy-start | bytes 2949124
  15.1 1.1 copy-start.13
  18.0 14.9 %all-to-all-start = ((bf16[8,2,3,2,1024]{4,3,2,1,0:T(2,128)(2,1)}), bf16[8,2,3,2,1024]{4,3,2,1,0:T(2,128)(2,1)}, u32[]{:S(2)}, u32[]{:S(2)}) async-start(bf16[8,2,3,2,1024]{4,3,2,1,0:T(2,128)(2,1)} %gather_fusion), calls=%async_computation | async-start | bytes 393216 | tf_op jit(solution)/shard_map/all_to_all | solution.py:24
  26.6 2.4 copy-start.2
  32.9 22.6 %all-to-all-start.1 = ((f32[8,2,16,1024]{3,2,1,0:T(8,128)}), f32[8,2,16,1024]{3,2,1,0:T(8,128)}, u32[]{:S(2)}, u32[]{:S(2)}) async-start(f32[8,2,16,1024]{3,2,1,0:T(8,128)} %gather_fusion.2), calls=%async_computation.1 | async-start | bytes 2097152 | tf_op jit(solution)/shard_map/all_to_all | solution.py:23
  47.4 8.2 %copy-start.5 = (f32[80,3,1024]{2,0,1:T(8,128)}, f32[80,3,1024]{2,0,1:T(8,128)S(1)}, u32[]{:S(2)}) copy-start(f32[80,3,1024]{2,0,1:T(8,128)S(1)} %get-tuple-element.23) | copy-start | bytes 2949124
  48.9 0.9 copy-start.15
  55.5 15.2 %all-to-all-start.2 = ((bf16[8,2,3,2,1024]{4,1,2,3,0:T(2,128)(2,1)}), bf16[8,2,3,2,1024]{4,1,2,3,0:T(2,128)(2,1)}, u32[]{:S(2)}, u32[]{:S(2)}) async-start(bf16[8,2,3,2,1024]{4,1,2,3,0:T(2,128)(2,1)} %gather_fusion.4), calls=%async_computation.2 | async-start | bytes 393216 | tf_op jit(solution)/shard_map/all_to_all | solution.py:24
  64.4 2.4 copy-start
  70.7 23.7 %all-to-all-start.3 = ((f32[8,2,16,1024]{3,2,1,0:T(8,128)}), f32[8,2,16,1024]{3,2,1,0:T(8,128)}, u32[]{:S(2)}, u32[]{:S(2)}) async-start(f32[8,2,16,1024]{3,2,1,0:T(8,128)} %gather_fusion.6), calls=%async_computation.3 | async-start | bytes 2097152 | tf_op jit(solution)/shard_map/all_to_all | solution.py:23
  86.7 7.7 %copy-start.14 = (bf16[80,3,2,1024]{3,0,1,2:T(8,128)(2,1)}, bf16[80,3,2,1024]{3,0,1,2:T(8,128)(2,1)S(1)}, u32[]{:S(2)}) copy-start(bf16[80,3,2,1024]{3,0,1,2:T(8,128)(2,1)S(1)} %maximum_multiply_fusion.5) | copy-start | bytes 2949124
  94.4 15.2 %all-to-all-start.4 = ((bf16[8,2,3,2,1024]{4,3,2,1,0:T(2,128)(2,1)}), bf16[8,2,3,2,1024]{4,3,2,1,0:T(2,128)(2,1)S(1)}, u32[]{:S(2)}, u32[]{:S(2)}) async-start(bf16[8,2,3,2,1024]{4,3,2,1,0:T(2,128)(2,1)} %gather_fusion.8), calls=%async_computation.4 | async-start | bytes 393216 | tf_op jit(solution)/shard_map/all_to_all | solution.py:24
  103.2 2.4 copy-start.1
  109.6 19.7 %all-to-all-start.5 = ((f32[8,2,16,1024]{3,2,1,0:T(8,128)}), f32[8,2,16,1024]{3,2,1,0:T(8,128)}, u32[]{:S(2)}, u32[]{:S(2)}) async-start(f32[8,2,16,1024]{3,2,1,0:T(8,128)} %gather_fusion.10), calls=%async_computation.5 | async-start | bytes 2097152 | tf_op jit(solution)/shard_map/all_to_all | solution.py:23
  113.9 238.3 %all-reduce.3.cloned.1.call-start = ((), (), s32[]{:S(2)}) async-start(), calls=%async_computation.6 | async-start | bytes 10485760 | tf_op jit(solution)/shard_map/psum | solution.py:62
  119.6 0.9 copy-start.8
  121.4 10.8 %copy-start.4 = (f32[80,1024]{1,0:T(8,128)S(1)}, f32[80,1024]{1,0:T(8,128)}, u32[]{:S(2)}) copy-start(f32[80,1024]{1,0:T(8,128)} %fusion.26) | copy-start | bytes 983044
  121.4 10.8 %copy-start.21 = (f32[16,1024]{1,0:T(8,128)S(1)}, f32[16,1024]{1,0:T(8,128)}, u32[]{:S(2)}) copy-start(f32[16,1024]{1,0:T(8,128)} %param.16) | copy-start | bytes 196612
  132.2 12.4 %copy-start.9 = (f32[80,3,1024]{2,0,1:T(8,128)S(1)}, f32[80,3,1024]{2,0,1:T(8,128)}, u32[]{:S(2)}) copy-start(f32[80,3,1024]{2,0,1:T(8,128)} %copy-done.8) | copy-start | bytes 2949124
  132.2 12.4 %copy-start.12 = (f32[80,1024]{1,0:T(8,128)S(1)}, f32[80,1024]{1,0:T(8,128)}, u32[]{:S(2)}) copy-start(f32[80,1024]{1,0:T(8,128)} %fusion.20) | copy-start | bytes 983044
  132.2 12.4 %copy-start.20 = (f32[1024]{0:T(1024)S(1)}, f32[1024]{0:T(1024)}, u32[]{:S(2)}) copy-start(f32[1024]{0:T(1024)} %param.17) | copy-start | bytes 12292
  144.6 6.2 %copy-start.7 = (f32[80,3,1024]{2,0,1:T(8,128)S(1)}, f32[80,3,1024]{2,0,1:T(8,128)}, u32[]{:S(2)}) copy-start(f32[80,3,1024]{2,0,1:T(8,128)} %get-tuple-element.21) | copy-start | bytes 2949124
  144.6 12.4 %slice-start = ((s8[8388608]{0:T(1024)(128)(4,1)}), s8[4194304]{0:T(1024)(128)(4,1)S(1)}, s32[]{:S(2)}) async-start(s8[8388608]{0:T(1024)(128)(4,1)} %bitcast.153), calls=%async_computation.7 | async-start | bytes 8388608
  150.9 6.2 %slice-start.1 = ((s8[8388608]{0:T(1024)(128)(4,1)}), s8[4194304]{0:T(1024)(128)(4,1)S(1)}, s32[]{:S(2)}) async-start(s8[8388608]{0:T(1024)(128)(4,1)} %bitcast.153), calls=%async_computation.8 | async-start | bytes 8388608
  150.9 6.2 %copy-start.11 = (f32[80,3,1024]{2,0,1:T(8,128)S(1)}, f32[80,3,1024]{2,0,1:T(8,128)}, u32[]{:S(2)}) copy-start(f32[80,3,1024]{2,0,1:T(8,128)} %copy-done.10) | copy-start | bytes 2949124
  157.0 2.7 copy-start.6
  162.4 1.0 copy-start.17
  162.4 1.2 copy-start.18
  162.4 195.9 %copy-start.22 = (f32[1024]{0:T(1024)S(1)}, f32[1024]{0:T(1024)}, u32[]{:S(2)}) copy-start(f32[1024]{0:T(1024)} %param.19) | copy-start | bytes 12292
Sparse Core Ops, SparseCore 0:
  162.5 189.6 all-reduce.2
where the time goes:
time: 369 us; the launch traced here: 368 us
  waiting for transfers between devices  190 us (51%)
  local copies, waits for them, and re-layouts  75.8 us (21%)
  other arithmetic  43.3 us (12%)
  starting transfers between devices  26.4 us (7%)
  matrix products  17.6 us (5%)
  between operations  14.5 us (4%)
    psum x1, waiting for transfers between devices, per_device(): summed = lax.psum(partial_out, 'tensor')  187 us
    dot_general x4, matrix products, per_device(): jnp.dot(gated_out, out_weight, preferred_element_type=jnp.float32)  17.6 us
    slice x3, local copies, waits for them, and re-layouts, migrate(): state_now = jnp.concatenate([new_state, state_now[band_rows:]], axis=0)  14.3 us
    all_to_all x3, starting transfers between devices, migrate(): lax.all_to_all(lag_bands[band_for], 'dp', split_axis=0, concat_axis=0, ti...  13.5 us
    unnamed x53, local copies, waits for them, and re-layouts  13.2 us
    all_to_all x3, starting transfers between devices, migrate(): lax.all_to_all(state_bands[band_for], 'dp', split_axis=0, concat_axis=0,...  12.7 us
    reduce_sum x1, other arithmetic, per_device(): jnp.sum(residues[None] * state_now, axis=1) + skip[None] * product  12.4 us
    mul x3, other arithmetic, migrate(): state_now = state_now * alive[:, None, None]  8.79 us
  transfers between devices with their start and end apart: 7, of which 2 were waited for; matrix products, arithmetic and copies ran while one was open for 20% of the time, Pallas kernels for 0%

commit v1 on v0

v1 whole, which is shorter than its diff:
```python
import functools

import jax
import jax.numpy as jnp
from jax import lax
from jax.experimental import pallas as pl
from jax.experimental.pallas import tpu as pltpu
from jax.sharding import PartitionSpec as P

STEPS = 4
CAP = 2
MESH = pl.DeviceIdType.MESH
LANES = 512


def row_update(poles, res, skip, s, x, p):
    s = poles * s + p
    y = jnp.sum(res * s, axis=0, keepdims=True) + skip * p
    return s, x * y


def kernel(groups, shards, chunks, *refs):
    refs = list(refs)

    def take(count):
        got = refs[:count]
        del refs[:count]
        return got

    nc = len(chunks)
    q_ref, l_ref, qm_ref, lm_ref, tap_ref, tapm_ref, mask_ref = take(7)
    st_ref, pole_ref, res_ref, skip_ref, w_hbm, gain_ref = take(6)
    alive_ref, bandfor_ref, shift_ref = take(3)
    mix_refs, st_outs = take(nc), take(nc)
    (lag_out,) = take(1)
    s_refs = take(nc)
    w_ref, lagm, msend = take(3)
    mrecv = take(STEPS - 1)
    gm, xs, ps, ys = take(4)
    g_refs, p_refs, r_refs, t_refs = take(nc), take(nc), take(nc), take(nc)
    ss_own, ss_recv = take(2)
    load_sem, store_sem, ms_sem, mr_sem, rs_sem, rr_sem, ss_sem, sr_sem = take(8)
    sm = s_refs[0]
    me = lax.axis_index("dp")
    z = lax.axis_index("tensor")
    cols = gain_ref.shape[1]
    chans = pole_ref.shape[1]
    lanes = min(LANES, chans)
    blocks = [slice(i, i + lanes) for i in range(0, chans, lanes)]
    bands_m = chunks[0] // CAP
    firsts = [sum(chunks[:c]) for c in range(nc)]
    parity = lax.broadcasted_iota(jnp.int32, (8, lanes), 0) % 2

    barrier = pltpu.get_barrier_semaphore()

    @pl.loop(1, groups)
    def _(d):
        pl.semaphore_signal(barrier, inc=1, device_id={"dp": lax.rem(me + d, groups)}, device_id_type=MESH)

    @pl.loop(1, shards)
    def _(d):
        pl.semaphore_signal(barrier, inc=1, device_id={"tensor": lax.rem(z + d, shards)}, device_id_type=MESH)

    loads = [
        pltpu.make_async_copy(st_ref.at[pl.ds(firsts[c], chunks[c])], s_refs[c], load_sem.at[c])
        for c in range(nc)
    ]
    load_w = pltpu.make_async_copy(w_hbm, w_ref, load_sem.at[nc])
    stores = [pltpu.make_async_copy(s_refs[c], st_outs[c], store_sem.at[c]) for c in range(nc)]
    loads[0].start()
    loads[1].start()
    load_w.start()
    for load in loads[2:]:
        load.start()
    ss_own[...] = jnp.zeros_like(ss_own)

    def migration(turn, d):
        return pltpu.make_async_remote_copy(
            src_ref=msend.at[turn, d],
            dst_ref=mrecv[turn].at[d],
            send_sem=ms_sem.at[turn, d],
            recv_sem=mr_sem.at[turn, d],
            device_id={"dp": lax.rem(me + d, groups)},
            device_id_type=MESH,
        )

    def filtered(sl, q, one, two):
        return tapm_ref[0, :, sl] * q + tapm_ref[1, :, sl] * one + tapm_ref[2, :, sl] * two

    def moving_step(turn):
        @pl.loop(0, bands_m)
        def _(b):
            for sl in blocks:
                q = qm_ref[turn, b, :, sl]
                if turn == 0:
                    one = lm_ref[0, b, :, sl]
                    two = lm_ref[1, b, :, sl]
                    states = [sm[b * CAP + r, :, sl] for r in range(CAP)]
                else:
                    k = shift_ref[turn - 1, b]
                    states = [
                        mrecv[turn - 1][k, 16 * r : 16 * r + 16, sl].astype(jnp.float32)
                        for r in range(CAP)
                    ]
                    lags = mrecv[turn - 1][k, 32:48, sl].astype(jnp.float32)
                    one = lags[:8]
                    two = lags[8:]
                f = filtered(sl, q, one, two)
                for r in range(CAP):
                    p = f[2 + r : 3 + r] * f[4 + r : 5 + r]
                    s, g = row_update(
                        pole_ref[:, sl], res_ref[:, sl], skip_ref[:, sl], states[r], f[r : r + 1], p
                    )
                    gm[pl.ds(turn * chunks[0] + b * CAP + r, 1), sl] = g
                    if turn < STEPS - 1:
                        s = s * alive_ref[turn, b * CAP + r]
                    sm[b * CAP + r, :, sl] = s
                if turn < STEPS - 1:
                    mask = jnp.where(
                        parity == 0, alive_ref[turn, b * CAP], alive_ref[turn, b * CAP + 1]
                    )
                    lagm[b, 0:8, sl] = q * mask
                    lagm[b, 8:16, sl] = one * mask
                else:
                    lag_out[b, :, sl] = one

    def pack(turn, d, to_ref):
        b = bandfor_ref[turn, d]
        for r in range(CAP):
            to_ref[16 * r : 16 * r + 16, :] = sm[b * CAP + r].astype(jnp.bfloat16)
        to_ref[32:48, :] = lagm[b].astype(jnp.bfloat16)

    def send_moving(turn):
        pack(turn, 0, mrecv[turn].at[0])

        @pl.loop(1, groups)
        def _(d):
            pack(turn, d, msend.at[turn, d])
            migration(turn, d).start()

    def await_moving(turn):
        @pl.loop(1, groups)
        def _(d):
            migration(turn, d).wait_recv()

    def staying(c):
        rows, first, s_ref, g_ref = chunks[c], firsts[c], s_refs[c], g_refs[c]

        @pl.loop(0, rows // 16)
        def _(i):
            at = pl.multiple_of(first + i * 16, 16)
            lag_at = pl.multiple_of(at - chunks[0], 16)

            @pl.loop(0, chans // 128)
            def _(block):
                sl = pl.ds(pl.multiple_of(block * 128, 128), 128)
                one = [l_ref[0, j, pl.ds(lag_at, 16), sl].astype(jnp.float32) for j in range(3)]
                two = [l_ref[1, j, pl.ds(lag_at, 16), sl].astype(jnp.float32) for j in range(3)]
                for turn in range(STEPS):
                    q = [q_ref[turn, j, pl.ds(at, 16), sl].astype(jnp.float32) for j in range(3)]
                    f = [
                        tap_ref[j, 0:1, sl] * q[j]
                        + tap_ref[j, 1:2, sl] * one[j]
                        + tap_ref[j, 2:3, sl] * two[j]
                        for j in range(3)
                    ]
                    xs[turn, :, sl] = f[0]
                    ps[turn, :, sl] = f[1] * f[2]
                    if turn < STEPS - 1:
                        mask = mask_ref[turn, pl.ds(at, 16), :]
                        two = [v * mask for v in one]
                        one = [v * mask for v in q]

            @pl.loop(0, 16)
            def _(r):
                for sl in blocks:
                    s = s_ref[i * 16 + r, :, sl]
                    for turn in range(STEPS):
                        s = pole_ref[:, sl] * s + ps[turn, pl.ds(r, 1), sl]
                        ys[turn, pl.ds(r, 1), sl] = jnp.sum(res_ref[:, sl] * s, axis=0, keepdims=True)
                        if turn < STEPS - 1:
                            s = s * alive_ref[turn, at + r]
                    s_ref[i * 16 + r, :, sl] = s

            for turn in range(STEPS):
                g_ref[pl.ds(pl.multiple_of(turn * rows + i * 16, 16), 16), :] = (
                    xs[turn] * (ys[turn] + skip_ref[...] * ps[turn])
                ).astype(jnp.bfloat16)

    def part_copy(c, j):
        return pltpu.make_async_remote_copy(
            src_ref=p_refs[c].at[j],
            dst_ref=r_refs[c].at[j],
            send_sem=rs_sem.at[c, j],
            recv_sem=rr_sem.at[c, j],
            device_id={"tensor": lax.rem(z + j, shards)},
            device_id_type=MESH,
        )

    def project(c):
        g_ref, p_ref, t_ref = g_refs[c], p_refs[c], t_refs[c]

        def product(j):
            owner = lax.rem(z + j, shards)
            return jnp.dot(
                g_ref[...],
                w_ref[:, pl.ds(pl.multiple_of(owner * cols, cols), cols)],
                preferred_element_type=jnp.float32,
            )

        @pl.loop(1, shards)
        def _(j):
            p_ref[j] = product(j).astype(jnp.bfloat16)
            part_copy(c, j).start()

        t_ref[...] = product(0)

    def pieces(rows):
        return [(i, min(128, rows - i)) for i in range(0, rows, 128)]

    def eye(size):
        return lax.broadcasted_iota(jnp.int32, (size, 128), 0) == lax.broadcasted_iota(
            jnp.int32, (size, 128), 1
        )

    def square_copy(c, j):
        return pltpu.make_async_remote_copy(
            src_ref=ss_own.at[c],
            dst_ref=ss_recv.at[c, j],
            send_sem=ss_sem.at[c, j],
            recv_sem=sr_sem.at[c, j],
            device_id={"tensor": lax.rem(z + j, shards)},
            device_id_type=MESH,
        )

    def collect(c):
        r_ref, t_ref = r_refs[c], t_refs[c]
        for j in range(1, shards):
            part_copy(c, j).wait_recv()
        for at, (i, size) in enumerate(pieces(t_ref.shape[0])):
            x = t_ref[i : i + size, :]
            for j in range(1, shards):
                x = x + r_ref[j, i : i + size, :].astype(jnp.float32)
            t_ref[i : i + size, :] = x
            squares = jnp.sum(x * x, axis=1, keepdims=True)
            ss_own[c, at : at + 1, :] = jnp.sum(
                jnp.where(eye(size), squares, 0.0), axis=0, keepdims=True
            )
        for j in range(1, shards):
            square_copy(c, j).start()

    def finish(c):
        t_ref, out_ref = t_refs[c], mix_refs[c]
        for j in range(1, shards):
            square_copy(c, j).wait_recv()
        total = ss_own[c]
        for j in range(1, shards):
            total = total + ss_recv[c, j]
        for at, (i, size) in enumerate(pieces(t_ref.shape[0])):
            squares = jnp.sum(jnp.where(eye(size), total[at : at + 1], 0.0), axis=1, keepdims=True)
            scale = lax.rsqrt(squares / (cols * shards) + 1e-05)
            out_ref[i : i + size, :] = (t_ref[i : i + size, :] * scale * gain_ref[...]).astype(
                jnp.bfloat16
            )

    def stay(c):
        loads[c].wait()
        staying(c)
        stores[c].start()
        if c == 1:
            load_w.wait()
        project(c)

    loads[0].wait()
    moving_step(0)
    pl.semaphore_wait(barrier, groups + shards - 2)
    send_moving(0)
    stay(1)
    await_moving(0)
    moving_step(1)
    send_moving(1)
    for c in range(2, nc):
        stay(c)
    await_moving(1)
    moving_step(2)
    send_moving(2)
    await_moving(2)
    moving_step(3)
    stores[0].start()
    g_refs[0][...] = gm[...].astype(jnp.bfloat16)
    project(0)
    for c in range(1, nc):
        collect(c)
    for c in range(1, nc):
        finish(c)
    collect(0)
    finish(0)
    for turn in range(STEPS - 1):
        @pl.loop(1, groups)
        def _(d):
            migration(turn, d).wait_send()
    for j in range(1, shards):
        for c in range(nc):
            part_copy(c, j).wait_send()
            square_copy(c, j).wait_send()
    for store in stores:
        store.wait()


def per_device(
    qkv,
    fir_buffer,
    fir_taps,
    modal_state,
    poles,
    residues,
    skip,
    out_weight,
    norm_gain,
    finished,
    dest_group,
):
    groups = lax.axis_size("dp")
    shards = lax.axis_size("tensor")
    rows, order, chans = modal_state.shape
    cols = norm_gain.shape[0]
    me = lax.axis_index("dp")
    f32 = jnp.float32
    bf16 = jnp.bfloat16

    moving = groups * CAP
    q_bands = qkv[:, :moving].reshape(STEPS, groups, CAP, 3, chans).transpose(0, 1, 3, 2, 4)
    q_bands = q_bands.reshape(STEPS, groups, 3 * CAP, chans).astype(f32)
    q_bands = jnp.pad(q_bands, ((0, 0), (0, 0), (0, 2), (0, 0)))
    l_bands = fir_buffer[:moving].reshape(groups, CAP, 3, 2, chans).transpose(3, 0, 2, 1, 4)
    l_bands = l_bands.reshape(2, groups, 3 * CAP, chans).astype(f32)
    l_bands = jnp.pad(l_bands, ((0, 0), (0, 0), (0, 2), (0, 0)))
    taps = jnp.repeat(fir_taps.transpose(1, 0, 2), CAP, axis=1)
    taps = jnp.pad(taps, ((0, 0), (0, 2), (0, 0)))
    alive = (1 - finished).astype(f32)
    mask = jnp.broadcast_to(alive[:, :, None], alive.shape + (128,))
    shift = (dest_group[:, 0:moving:CAP] - me + groups) % groups
    ids = jnp.arange(groups, dtype=jnp.int32)
    bandfor = jnp.sum(jnp.where(shift[:, None, :] == ids[None, :, None], ids[None, None, :], 0), axis=2)

    left = rows - moving
    half = left // 32 * 16
    chunks = (moving,) + ((half, left - half) if half else (left,))
    nc = len(chunks)
    tall = [STEPS * n for n in chunks]
    vmem = pl.BlockSpec(memory_space=pltpu.VMEM)
    smem = pl.BlockSpec(memory_space=pltpu.SMEM)
    hbm = pl.BlockSpec(memory_space=pl.ANY)
    dma = pltpu.SemaphoreType.DMA
    outs = pl.pallas_call(
        functools.partial(kernel, groups, shards, chunks),
        out_shape=[jax.ShapeDtypeStruct((n, cols), bf16) for n in tall]
        + [jax.ShapeDtypeStruct((n, order, chans), f32) for n in chunks]
        + [jax.ShapeDtypeStruct((groups, 8, chans), f32)],
        in_specs=[vmem] * 7 + [hbm, vmem, vmem, vmem, hbm, vmem, smem, smem, smem],
        out_specs=[vmem] * nc + [hbm] * nc + [vmem],
        scratch_shapes=[pltpu.VMEM((n, order, chans), f32) for n in chunks]
        + [
            pltpu.VMEM(out_weight.shape, bf16),
            pltpu.VMEM((groups, 16, chans), f32),
            pltpu.VMEM((STEPS - 1, groups, 48, chans), bf16),
        ]
        + [pltpu.VMEM((groups, 48, chans), bf16)] * (STEPS - 1)
        + [pltpu.VMEM((tall[0], chans), f32)]
        + [pltpu.VMEM((STEPS, 16, chans), f32)] * 3
        + [pltpu.VMEM((n, chans), bf16) for n in tall]
        + [pltpu.VMEM((shards, n, cols), bf16) for n in tall]
        + [pltpu.VMEM((shards, n, cols), bf16) for n in tall]
        + [pltpu.VMEM((n, cols), f32) for n in tall]
        + [
            pltpu.VMEM((nc, 8, 128), f32),
            pltpu.VMEM((nc, shards, 8, 128), f32),
            dma((nc + 1,)),
            dma((nc,)),
            dma((STEPS - 1, groups)),
            dma((STEPS - 1, groups)),
            dma((nc, shards)),
            dma((nc, shards)),
            dma((nc, shards)),
            dma((nc, shards)),
        ],
        compiler_params=pltpu.CompilerParams(
            collective_id=0, has_side_effects=True, vmem_limit_bytes=56 * 1024 * 1024
        ),
        name="mixer",
    )(
        qkv.transpose(0, 2, 1, 3),
        fir_buffer[moving:].transpose(2, 1, 0, 3),
        q_bands,
        l_bands,
        fir_taps,
        taps,
        mask,
        modal_state,
        poles,
        residues,
        skip[None],
        out_weight,
        norm_gain[None],
        alive,
        bandfor.astype(jnp.int32),
        shift.astype(jnp.int32),
    )
    mixed = jnp.concatenate([o.reshape(STEPS, -1, cols) for o in outs[:nc]], axis=1)
    state = jnp.concatenate(outs[nc : 2 * nc], axis=0)
    moved = outs[2 * nc][:, : 3 * CAP].reshape(groups, 3, CAP, chans).transpose(0, 2, 1, 3)
    moved = moved.reshape(moving, 3, chans).astype(bf16)
    stayed = qkv[2, moving:] * alive[2, moving:].astype(bf16)[:, None, None]
    lagged = jnp.stack([qkv[3], jnp.concatenate([moved, stayed], axis=0)], axis=2)
    return (mixed, state, lagged)


def solution(mesh):
    return jax.shard_map(
        per_device,
        mesh=mesh,
        in_specs=(
            P(None, "dp", None, "tensor"),
            P("dp", None, None, "tensor"),
            P(None, None, "tensor"),
            P("dp", None, "tensor"),
            P(None, "tensor"),
            P(None, "tensor"),
            P("tensor"),
            P("tensor", None),
            P("tensor"),
            P(None, "dp"),
            P(None, "dp"),
        ),
        out_specs=(P(None, "dp", "tensor"), P("dp", None, "tensor"), P("dp", None, None, "tensor")),
        check_vma=False,
    )
```

time: 369 us -> 97.1 us (0.26)
  waiting for transfers between devices: 190 us -> 0 us
  Pallas kernels: 0 us -> 76.1 us
  local copies, waits for them, and re-layouts: 75.8 us -> 8.68 us
  other arithmetic: 43.3 us -> 11.2 us
  starting transfers between devices: 26.4 us -> 0 us
  matrix products: 17.6 us -> 0 us
  between operations: 14.5 us -> 0.81 us
    psum x1 -> x0, waiting for transfers between devices: 187 us -> none  [per_device(): summed = lax.psum(partial_out, 'tensor')]
    pallas_call x0 -> x1, Pallas kernels: none -> 76.1 us  [per_device(): pl.pallas_call(functools.partial(kernel, groups, shards, chunks), out_sha...]
    gather x13 -> x0, local copies, waits for them, and re-layouts: 27.9 us -> none  [the longest x3 8.58 us: migrate(): state_bands[band_for]]
    all_to_all x6 -> x0, starting transfers between devices: 26.2 us -> none  [the longest x3 13.5 us: migrate(): lax.all_to_all(lag_bands[band_for], 'dp', split_axis=0, concat_axis=0, ti...]
    slice x19 -> x9, local copies, waits for them, and re-layouts: 27.7 us -> 2.19 us  [the longest x2 1.33 us: per_device(): qkv[:, :moving].reshape(STEPS, groups, CAP, 3, chans)]
    reduce_sum x8 -> x1, other arithmetic: 18.8 us -> 0.73 us  [per_device(): jnp.sum(jnp.where(shift[:, None, :] == ids[None, :, None], ids[None, None...]
    dot_general x4 -> x0, matrix products: 17.6 us -> none  [per_device(): jnp.dot(gated_out, out_weight, preferred_element_type=jnp.float32)]
    mul x6 -> x1, other arithmetic: 11.7 us -> 1.09 us  [per_device(): stayed = qkv[2, moving:] * alive[2, moving:].astype(bf16)[:, None, None]]
  transfers between devices with their start and end apart: 7 -> 0, of which waited for: 2 -> 0; matrix products, arithmetic and copies ran while one was open for 20% -> 0% of each run, Pallas kernels for 0% -> 0%
where the time goes in v1:
time: 97.1 us; the launch traced here: 96.8 us
  Pallas kernels  76.1 us (78%)
  other arithmetic  11.2 us (12%)
  local copies, waits for them, and re-layouts  8.68 us (9%)
    pallas_call x1, Pallas kernels, per_device(): pl.pallas_call(functools.partial(kernel, groups, shards, chunks), out_sha...  76.1 us
    concatenate x1, other arithmetic, per_device(): state = jnp.concatenate(outs[nc:2 * nc], axis=0)  5.77 us
    unnamed x16, local copies, waits for them, and re-layouts  3.07 us

profile of v1, /device:TPU:0, one launch (start us, length us, event | category | flops | bytes accessed | tf_op | source)
XLA Modules:
  0.0 96.8 jit_solution(4162050256182397792)
XLA Ops:
  0.6 0.7 fusion.1
  1.3 0.7 broadcast_in_dim.32.refs_6_
  2.1 0.8 slice.29
  2.8 0.7 select_reduce_fusion.refs_14_
  3.6 1.0 %slice.27 = bf16[4,16,3,1024]{3,1,2,0:T(8,128)(2,1)S(1)} slice(bf16[4,80,3,1024]{3,1,2,0:T(8,128)(2,1)} %param.11), slice={[0:4], [0:16], [0:3], [0:1024]} | slice | bytes 786432 | tf_op jit(solution)/shard_map/slice | solution.py:332
  4.6 0.3 copy.38
  4.9 0.2 copy.39
  5.1 0.0 slice-start
  5.2 0.2 copy.40
  5.4 1.1 %pad_convert_fusion.refs_2_ = f32[4,8,8,1024]{3,2,1,0:T(8,128)} fusion(bf16[4,8,6,1024]{3,2,1,0:T(8,128)(2,1)S(1)} %copy.40), kind=kLoop, calls=%fused_computation.4 | loop fusion | flops 262144 | bytes 1441792 | tf_op jit(solution)/shard_map/jit(_pad)/pad | solution.py:334
  6.5 0.0 copy-done.6
  6.5 0.0 copy-start.2
  6.5 1.1 %copy.49 = bf16[64,3,2,1024]{3,0,1,2:T(8,128)(2,1)} copy(bf16[64,3,2,1024]{3,2,1,0:T(2,128)(2,1)S(1)} %slice-done) | data formatting | bytes 1572864
  7.6 0.1 copy.41
  7.7 0.1 copy.42
  7.8 0.8 pad_convert_fusion.1.refs_3_
  8.7 0.1 reshape.42
  8.8 0.7 pad.20.refs_5_
  9.4 76.1 %mixer.1 = (bf16[64,1024]{1,0:T(8,128)(2,1)}, bf16[128,1024]{1,0:T(8,128)(2,1)}, bf16[128,1024]{1,0:T(8,128)(2,1)}, f32[16,16,1024]{2,1,0:T(8,128)}, f32[32,16,1...) custom-call(bf16[4,3,80,1024]{3,2,1,0:T(8,128)(2,1)} %bitcast.31, bf16[2,3,64,1024]{3,2,1,0:T(8,128)(2,1)} %bitcast.32, ...), custom_call_target="tpu_custom_call" | custom-call | tf_op jit(solution)/shard_map/mixer/pallas_call | solution.py:355
  85.5 0.0 copy-start
  85.5 0.0 copy-start.1
  85.5 0.0 copy-start.3
  85.5 0.0 copy-start.4
  85.5 5.8 %pad_maximum_fusion = f32[80,16,1024]{2,1,0:T(8,128)} fusion(f32[32,16,1024]{2,1,0:T(8,128)} %get-tuple-element.15, f32[32,16,1024]{2,1,0:T(8,128)} %get-tuple-element.14, f32[16,16,1024]{2,1,0:T(8,128)} %get-tuple-element.13), kind=kLoop, calls=%fused_computation | loop fusion | flops 2621440 | bytes 10485760 | tf_op jit(solution)/shard_map/concatenate | solution.py:410
  91.3 0.9 pad_maximum_fusion.2
  92.2 0.1 copy.44
  92.3 0.1 copy.45
  92.5 0.1 slice_bitcast_fusion.1
  92.5 1.1 %bitcast_multiply_fusion = bf16[64,3,1024]{2,0,1:T(8,128)(2,1)S(1)} fusion(bf16[4,80,3,1024]{3,1,2,0:T(8,128)(2,1)} %param.11, bf16[64]{0:T(256)(128)(2,1)S(1)} %slice_bitcast_fusion.1), kind=kLoop, calls=%fused_computation.7 | loop fusion | flops 196608 | bytes 786560 | tf_op jit(solution)/shard_map/mul | solution.py:413
  93.7 1.1 %slice_bitcast_fusion = bf16[80,3,1,1024]{3,0,2,1:T(8,128)(2,1)S(1)} fusion(bf16[4,80,3,1024]{3,1,2,0:T(8,128)(2,1)} %param.11), kind=kLoop, calls=%fused_computation.6 | loop fusion | bytes 983040 | tf_op jit(solution)/shard_map/stack;squeeze | solution.py:414
  94.7 0.1 pad_maximum_fusion.1
  94.8 2.0 %copy.46 = bf16[80,3,2,1024]{3,2,1,0:T(2,128)(2,1)} copy(bf16[80,3,2,1024]{3,0,2,1:T(8,128)(2,1)S(1)} %pad_maximum_fusion.1) | data formatting | bytes 1966080
  (17 shorter events, 0.2 us)
Async XLA Ops:
  1.3 5.2 %copy-start.5 = (f32[3,80]{1,0:T(4,128)}, f32[3,80]{1,0:T(4,128)S(1)}, u32[]{:S(2)}) copy-start(f32[3,80]{1,0:T(4,128)S(1)} %get-tuple-element.27.refs_13_) | copy-start | bytes 2884
  2.8 3.6 %copy-start.6 = (s32[3,8]{1,0:T(4,128)}, s32[3,8]{1,0:T(4,128)S(1)}, u32[]{:S(2)}) copy-start(s32[3,8]{1,0:T(4,128)S(1)} %add_select_fusion.refs_15_) | copy-start | bytes 292
  5.1 1.3 %slice-start = ((bf16[80,3,2,1024]{3,2,1,0:T(2,128)(2,1)}), bf16[64,3,2,1024]{3,2,1,0:T(2,128)(2,1)S(1)}, s32[]{:S(2)}) async-start(bf16[80,3,2,1024]{3,2,1,0:T(2,128)(2,1)} %param.12), calls=%async_computation | async-start | bytes 1572864 | tf_op jit(solution)/shard_map/slice | solution.py:393
  6.5 1.1 %slice-start.1 = ((bf16[80,3,2,1024]{3,2,1,0:T(2,128)(2,1)}), bf16[16,3,2,1024]{3,2,1,0:T(2,128)(2,1)S(1)}, s32[]{:S(2)}) async-start(bf16[80,3,2,1024]{3,2,1,0:T(2,128)(2,1)} %param.12), calls=%async_computation.1 | async-start | bytes 393216 | tf_op jit(solution)/shard_map/slice | solution.py:335
  6.5 2.1 %copy-start.2 = (f32[3,3,1024]{2,1,0:T(4,128)S(1)}, f32[3,3,1024]{2,1,0:T(4,128)}, u32[]{:S(2)}) copy-start(f32[3,3,1024]{2,1,0:T(4,128)} %refs_4_.1) | copy-start | bytes 110596
  85.5 5.8 %copy-start = (bf16[128,1024]{1,0:T(8,128)(2,1)S(1)}, bf16[128,1024]{1,0:T(8,128)(2,1)}, u32[]{:S(2)}) copy-start(bf16[128,1024]{1,0:T(8,128)(2,1)} %get-tuple-element.11) | copy-start | bytes 786436
  85.5 5.8 %copy-start.1 = (bf16[128,1024]{1,0:T(8,128)(2,1)S(1)}, bf16[128,1024]{1,0:T(8,128)(2,1)}, u32[]{:S(2)}) copy-start(bf16[128,1024]{1,0:T(8,128)(2,1)} %get-tuple-element.12) | copy-start | bytes 786436
  85.5 5.8 %copy-start.3 = (bf16[64,1024]{1,0:T(8,128)(2,1)S(1)}, bf16[64,1024]{1,0:T(8,128)(2,1)}, u32[]{:S(2)}) copy-start(bf16[64,1024]{1,0:T(8,128)(2,1)} %get-tuple-element.10) | copy-start | bytes 393220
  85.5 6.7 %copy-start.4 = (f32[8,8,1024]{2,1,0:T(8,128)S(1)}, f32[8,8,1024]{2,1,0:T(8,128)}, u32[]{:S(2)}) copy-start(f32[8,8,1024]{2,1,0:T(8,128)} %get-tuple-element.16) | copy-start | bytes 786436

commit v2 on v1

v2 whole, which is shorter than its diff:
```python
import functools

import jax
import jax.numpy as jnp
from jax import lax
from jax.experimental import pallas as pl
from jax.experimental.pallas import tpu as pltpu
from jax.sharding import PartitionSpec as P

STEPS = 4
CAP = 2
MESH = pl.DeviceIdType.MESH
LANES = 512


def row_update(poles, res, skip, s, x, p):
    s = poles * s + p
    y = jnp.sum(res * s, axis=0, keepdims=True) + skip * p
    return s, x * y


def kernel(groups, shards, chunks, *refs):
    refs = list(refs)

    def take(count):
        got = refs[:count]
        del refs[:count]
        return got

    nc = len(chunks)
    q_ref, l_ref, tap_ref, fin_ref = take(4)
    st_ref, pole_ref, res_ref, skip_ref, w_hbm, gain_ref = take(6)
    done_ref, dest_ref = take(2)
    mix_out, st_out, lag_out = take(3)
    s_refs = take(nc)
    w_ref, lagn, lagm, msend = take(4)
    mrecv = take(STEPS - 1)
    xm, pm, ym, xs, ps, ys = take(6)
    g_refs, p_refs, r_refs, relay_refs, t_refs = take(nc), take(nc), take(nc), take(nc), take(nc)
    ss_own, ss_recv = take(2)
    load_sem, store_sem, ms_sem, mr_sem, rs_sem, rr_sem, rl_sem, ss_sem, sr_sem = take(9)
    sm = s_refs[0]
    me = lax.axis_index("dp")
    z = lax.axis_index("tensor")
    cols = gain_ref.shape[1]
    chans = pole_ref.shape[1]
    lanes = min(LANES, chans)
    blocks = [slice(i, i + lanes) for i in range(0, chans, lanes)]
    bands_m = chunks[0] // CAP
    firsts = [sum(chunks[:c]) for c in range(nc)]

    barrier = pltpu.get_barrier_semaphore()

    @pl.loop(1, groups)
    def _(d):
        pl.semaphore_signal(barrier, inc=1, device_id={"dp": lax.rem(me + d, groups)}, device_id_type=MESH)

    @pl.loop(1, shards)
    def _(d):
        pl.semaphore_signal(barrier, inc=1, device_id={"tensor": lax.rem(z + d, shards)}, device_id_type=MESH)

    loads = [
        pltpu.make_async_copy(st_ref.at[pl.ds(firsts[c], chunks[c])], s_refs[c], load_sem.at[c])
        for c in range(nc)
    ]
    load_w = pltpu.make_async_copy(w_hbm, w_ref, load_sem.at[nc])
    stores = [
        pltpu.make_async_copy(s_refs[c], st_out.at[pl.ds(firsts[c], chunks[c])], store_sem.at[c])
        for c in range(nc)
    ]
    loads[0].start()
    loads[1].start()
    load_w.start()
    for load in loads[2:]:
        load.start()
    ss_own[...] = jnp.zeros_like(ss_own)
    lagm[...] = jnp.zeros_like(lagm)

    def migration(turn, d):
        return pltpu.make_async_remote_copy(
            src_ref=msend.at[turn, d],
            dst_ref=mrecv[turn].at[d],
            send_sem=ms_sem.at[turn, d],
            recv_sem=mr_sem.at[turn, d],
            device_id={"dp": lax.rem(me + d, groups)},
            device_id_type=MESH,
        )

    def alive(turn, row):
        return (1 - done_ref[turn, row]).astype(jnp.float32)

    def alive_column(turn, at):
        shape = (16, fin_ref.shape[1])
        row = lax.broadcasted_iota(jnp.int32, shape, 0) + at
        lane = lax.broadcasted_iota(jnp.int32, shape, 1)
        flags = (1 - fin_ref[turn : turn + 1, :]).astype(jnp.float32)
        return jnp.sum(jnp.where(row == lane, flags, 0.0), axis=1, keepdims=True)

    def taken(sl, q, one, two):
        return [
            tap_ref[j, 0:1, sl] * q[j] + tap_ref[j, 1:2, sl] * one[j] + tap_ref[j, 2:3, sl] * two[j]
            for j in range(3)
        ]

    def moving_step(turn):
        if turn > 0:
            @pl.loop(0, chunks[0] // 8)
            def _(i):
                lags = []
                for u in range(8 // CAP):
                    k = lax.rem(dest_ref[turn - 1, i * 8 + u * CAP] - me + groups, groups)
                    lags.append(mrecv[turn - 1][k, 32:48, :].astype(jnp.float32))
                for l in range(2):
                    for j in range(3):
                        at = l * 8 + j * CAP
                        lagn[l, j, pl.ds(pl.multiple_of(i * 8, 8), 8), :] = jnp.concatenate(
                            [lag[at : at + CAP] for lag in lags], axis=0
                        )

        @pl.loop(0, chunks[0] // 16)
        def _(i):
            rows = pl.ds(pl.multiple_of(i * 16, 16), 16)
            mask = alive_column(turn, i * 16) if turn < STEPS - 1 else None

            @pl.loop(0, chans // 128)
            def _(block):
                sl = pl.ds(pl.multiple_of(block * 128, 128), 128)
                lag_ref = lagn if turn > 0 else l_ref
                one = [lag_ref[0, j, rows, sl].astype(jnp.float32) for j in range(3)]
                two = [lag_ref[1, j, rows, sl].astype(jnp.float32) for j in range(3)]
                q = [q_ref[turn, j, rows, sl].astype(jnp.float32) for j in range(3)]
                f = taken(sl, q, one, two)
                xm[rows, sl] = f[0]
                pm[rows, sl] = f[1] * f[2]
                for j in range(3):
                    if turn < STEPS - 1:
                        lagn[0, j, rows, sl] = q[j] * mask
                        lagn[1, j, rows, sl] = one[j] * mask
                    else:
                        lag_out[0, j, rows, sl] = q[j].astype(jnp.bfloat16)
                        lag_out[1, j, rows, sl] = one[j].astype(jnp.bfloat16)

        @pl.loop(0, bands_m)
        def _(b):
            if turn > 0:
                k = lax.rem(dest_ref[turn - 1, b * CAP] - me + groups, groups)
            for r in range(CAP):
                row = b * CAP + r
                for sl in blocks:
                    if turn > 0:
                        s = mrecv[turn - 1][k, 16 * r : 16 * r + 16, sl].astype(jnp.float32)
                    else:
                        s = sm[row, :, sl]
                    s = pole_ref[:, sl] * s + pm[pl.ds(row, 1), sl]
                    ym[pl.ds(row, 1), sl] = jnp.sum(res_ref[:, sl] * s, axis=0, keepdims=True)
                    if turn < STEPS - 1:
                        s = s * alive(turn, row)
                    sm[row, :, sl] = s

        if turn < STEPS - 1:
            @pl.loop(0, chunks[0] // 8)
            def _(i):
                for l in range(2):
                    for j in range(3):
                        at = l * 8 + j * CAP
                        lag = lagn[l, j, pl.ds(pl.multiple_of(i * 8, 8), 8), :]
                        for u in range(8 // CAP):
                            lagm[i * (8 // CAP) + u, at : at + CAP, :] = lag[u * CAP : u * CAP + CAP]

    def moving_gate(turn):
        g_refs[0][turn * chunks[0] : (turn + 1) * chunks[0], :] = (
            xm[...] * (ym[...] + skip_ref[...] * pm[...])
        ).astype(jnp.bfloat16)

    def pack(turn, d, to_ref):
        target = lax.rem(me + d, groups)
        b = lax.fori_loop(
            0,
            bands_m,
            lambda i, found: jnp.where(dest_ref[turn, i * CAP] == target, i, found),
            jnp.int32(0),
        )
        for r in range(CAP):
            to_ref[16 * r : 16 * r + 16, :] = sm[b * CAP + r].astype(jnp.bfloat16)
        to_ref[32:48, :] = lagm[b].astype(jnp.bfloat16)

    def send_moving(turn):
        pack(turn, 0, mrecv[turn].at[0])

        @pl.loop(1, groups)
        def _(d):
            pack(turn, d, msend.at[turn, d])
            migration(turn, d).start()

    def await_moving(turn):
        @pl.loop(1, groups)
        def _(d):
            migration(turn, d).wait_recv()

    def staying(c):
        rows, first, s_ref, g_ref = chunks[c], firsts[c], s_refs[c], g_refs[c]

        @pl.loop(0, rows // 16)
        def _(i):
            at = pl.multiple_of(first + i * 16, 16)
            masks = [alive_column(turn, at) for turn in range(STEPS - 1)]

            @pl.loop(0, chans // 128)
            def _(block):
                sl = pl.ds(pl.multiple_of(block * 128, 128), 128)
                one = [l_ref[0, j, pl.ds(at, 16), sl].astype(jnp.float32) for j in range(3)]
                two = [l_ref[1, j, pl.ds(at, 16), sl].astype(jnp.float32) for j in range(3)]
                for turn in range(STEPS):
                    q = [q_ref[turn, j, pl.ds(at, 16), sl].astype(jnp.float32) for j in range(3)]
                    f = taken(sl, q, one, two)
                    xs[turn, :, sl] = f[0]
                    ps[turn, :, sl] = f[1] * f[2]
                    if turn < STEPS - 1:
                        two = [v * masks[turn] for v in one]
                        one = [v * masks[turn] for v in q]
                    else:
                        for j in range(3):
                            lag_out[0, j, pl.ds(at, 16), sl] = q[j].astype(jnp.bfloat16)
                            lag_out[1, j, pl.ds(at, 16), sl] = one[j].astype(jnp.bfloat16)

            @pl.loop(0, 16)
            def _(r):
                for sl in blocks:
                    s = s_ref[i * 16 + r, :, sl]
                    for turn in range(STEPS):
                        s = pole_ref[:, sl] * s + ps[turn, pl.ds(r, 1), sl]
                        ys[turn, pl.ds(r, 1), sl] = jnp.sum(res_ref[:, sl] * s, axis=0, keepdims=True)
                        if turn < STEPS - 1:
                            s = s * alive(turn, at + r)
                    s_ref[i * 16 + r, :, sl] = s

            for turn in range(STEPS):
                g_ref[pl.ds(pl.multiple_of(turn * rows + i * 16, 16), 16), :] = (
                    xs[turn] * (ys[turn] + skip_ref[...] * ps[turn])
                ).astype(jnp.bfloat16)

    def near_copy(c, s):
        gap = jnp.abs(s - z)
        slot = jnp.where(s > z, 0, 2) + jnp.minimum(gap, 2) - 1
        return pltpu.make_async_remote_copy(
            src_ref=p_refs[c].at[s],
            dst_ref=r_refs[c].at[slot],
            send_sem=rs_sem.at[c, s],
            recv_sem=rr_sem.at[c, slot],
            device_id={"tensor": s},
            device_id_type=MESH,
        )

    def far_copy(c, s):
        return pltpu.make_async_remote_copy(
            src_ref=p_refs[c].at[s],
            dst_ref=relay_refs[c].at[s],
            send_sem=rs_sem.at[c, s],
            recv_sem=rl_sem.at[c, s],
            device_id={"tensor": jnp.where(s > z, z + 1, z - 1)},
            device_id_type=MESH,
        )

    def send_part(c, s):
        gap = jnp.abs(s - z)

        @pl.when(gap <= 2)
        def _():
            near_copy(c, s).start()

        @pl.when(gap > 2)
        def _():
            far_copy(c, s).start()

    def owner_at(i):
        return jnp.where(2 * z < shards, shards - 1 - i, i)

    def relays(s):
        behind = jnp.where(s > z, z > 0, z < shards - 1)
        return jnp.logical_and(jnp.abs(s - z) >= 2, behind)

    def product(c, s):
        return jnp.dot(
            g_refs[c][...],
            w_ref[:, pl.ds(pl.multiple_of(s * cols, cols), cols)],
            preferred_element_type=jnp.float32,
        )

    def project(c):
        @pl.loop(0, shards)
        def _(i):
            s = owner_at(i)

            @pl.when(jnp.logical_and(s != z, jnp.logical_not(relays(s))))
            def _():
                p_refs[c][s] = product(c, s).astype(jnp.bfloat16)
                send_part(c, s)

        t_refs[c][...] = product(c, z)

    def relay(c):
        @pl.loop(0, shards)
        def _(i):
            s = owner_at(i)

            @pl.when(jnp.logical_and(s != z, relays(s)))
            def _():
                part = product(c, s)
                far_copy(c, s).wait_recv()
                p_refs[c][s] = (part + relay_refs[c][s].astype(jnp.float32)).astype(jnp.bfloat16)
                send_part(c, s)

    here = [z >= 1, z >= 2, z <= shards - 2, z <= shards - 3]

    def pieces(rows):
        return [(i, min(128, rows - i)) for i in range(0, rows, 128)]

    def eye(size):
        return lax.broadcasted_iota(jnp.int32, (size, 128), 0) == lax.broadcasted_iota(
            jnp.int32, (size, 128), 1
        )

    def square_copy(c, j):
        return pltpu.make_async_remote_copy(
            src_ref=ss_own.at[c],
            dst_ref=ss_recv.at[c, j],
            send_sem=ss_sem.at[c, j],
            recv_sem=sr_sem.at[c, j],
            device_id={"tensor": lax.rem(z + j, shards)},
            device_id_type=MESH,
        )

    def collect(c):
        r_ref, t_ref = r_refs[c], t_refs[c]
        for slot in range(4):
            @pl.when(here[slot])
            def _():
                pltpu.make_async_remote_copy(
                    src_ref=r_ref.at[slot],
                    dst_ref=r_ref.at[slot],
                    send_sem=rs_sem.at[c, 0],
                    recv_sem=rr_sem.at[c, slot],
                    device_id={"tensor": lax.rem(z + 1, shards)},
                    device_id_type=MESH,
                ).wait_recv()
                t_ref[...] += r_ref[slot].astype(jnp.float32)

        for at, (i, size) in enumerate(pieces(t_ref.shape[0])):
            x = t_ref[i : i + size, :]
            squares = jnp.sum(x * x, axis=1, keepdims=True)
            ss_own[c, at : at + 1, :] = jnp.sum(
                jnp.where(eye(size), squares, 0.0), axis=0, keepdims=True
            )
        for j in range(1, shards):
            square_copy(c, j).start()

    def finish(c):
        t_ref, rows, first = t_refs[c], chunks[c], firsts[c]
        for j in range(1, shards):
            square_copy(c, j).wait_recv()
        total = ss_own[c]
        for j in range(1, shards):
            total = total + ss_recv[c, j]
        for at, (i, size) in enumerate(pieces(t_ref.shape[0])):
            squares = jnp.sum(jnp.where(eye(size), total[at : at + 1], 0.0), axis=1, keepdims=True)
            scale = lax.rsqrt(squares / (cols * shards) + 1e-05)
            value = (t_ref[i : i + size, :] * scale * gain_ref[...]).astype(jnp.bfloat16)
            for turn in range(i // rows, (i + size) // rows):
                part = turn * rows - i
                mix_out[turn, first : first + rows, :] = value[part : part + rows]

    def stay(c):
        loads[c].wait()
        staying(c)
        stores[c].start()
        if c == 1:
            load_w.wait()
        project(c)

    loads[0].wait()
    moving_step(0)
    pl.semaphore_wait(barrier, groups + shards - 2)
    send_moving(0)
    moving_gate(0)
    stay(1)
    await_moving(0)
    moving_step(1)
    send_moving(1)
    moving_gate(1)
    relay(1)
    for c in range(2, nc):
        stay(c)
    await_moving(1)
    moving_step(2)
    send_moving(2)
    moving_gate(2)
    for c in range(2, nc):
        relay(c)
    await_moving(2)
    moving_step(3)
    moving_gate(3)
    stores[0].start()
    project(0)
    collect(1)
    relay(0)
    for c in range(2, nc):
        collect(c)
    for c in range(1, nc):
        finish(c)
    collect(0)
    finish(0)
    for turn in range(STEPS - 1):
        @pl.loop(1, groups)
        def _(d):
            migration(turn, d).wait_send()
    for c in range(nc):
        @pl.loop(0, shards)
        def _(s):
            @pl.when(s != z)
            def _():
                near_copy(c, s).wait_send()

        for j in range(1, shards):
            square_copy(c, j).wait_send()
    for store in stores:
        store.wait()


def per_device(
    qkv,
    fir_buffer,
    fir_taps,
    modal_state,
    poles,
    residues,
    skip,
    out_weight,
    norm_gain,
    finished,
    dest_group,
):
    groups = lax.axis_size("dp")
    shards = lax.axis_size("tensor")
    rows, order, chans = modal_state.shape
    cols = norm_gain.shape[0]
    f32 = jnp.float32
    bf16 = jnp.bfloat16

    moving = groups * CAP
    left = rows - moving
    half = left // 32 * 16
    chunks = (moving,) + ((half, left - half) if half else (left,))
    nc = len(chunks)
    tall = [STEPS * n for n in chunks]
    vmem = pl.BlockSpec(memory_space=pltpu.VMEM)
    smem = pl.BlockSpec(memory_space=pltpu.SMEM)
    hbm = pl.BlockSpec(memory_space=pl.ANY)
    dma = pltpu.SemaphoreType.DMA
    outs = pl.pallas_call(
        functools.partial(kernel, groups, shards, chunks),
        out_shape=[
            jax.ShapeDtypeStruct((STEPS, rows, cols), bf16),
            jax.ShapeDtypeStruct(modal_state.shape, f32),
            jax.ShapeDtypeStruct((2, 3, rows, chans), bf16),
        ],
        in_specs=[vmem] * 4 + [hbm, vmem, vmem, vmem, hbm, vmem, smem, smem],
        out_specs=[vmem, hbm, vmem],
        scratch_shapes=[pltpu.VMEM((n, order, chans), f32) for n in chunks]
        + [
            pltpu.VMEM(out_weight.shape, bf16),
            pltpu.VMEM((2, 3, moving, chans), f32),
            pltpu.VMEM((groups, 16, chans), f32),
            pltpu.VMEM((STEPS - 1, groups, 48, chans), bf16),
        ]
        + [pltpu.VMEM((groups, 48, chans), bf16)] * (STEPS - 1)
        + [pltpu.VMEM((moving, chans), f32)] * 3
        + [pltpu.VMEM((STEPS, 16, chans), f32)] * 3
        + [pltpu.VMEM((n, chans), bf16) for n in tall]
        + [pltpu.VMEM((shards, n, cols), bf16) for n in tall]
        + [pltpu.VMEM((4, n, cols), bf16) for n in tall]
        + [pltpu.VMEM((shards, n, cols), bf16) for n in tall]
        + [pltpu.VMEM((n, cols), f32) for n in tall]
        + [
            pltpu.VMEM((nc, 8, 128), f32),
            pltpu.VMEM((nc, shards, 8, 128), f32),
            dma((nc + 1,)),
            dma((nc,)),
            dma((STEPS - 1, groups)),
            dma((STEPS - 1, groups)),
            dma((nc, shards)),
            dma((nc, 4)),
            dma((nc, shards)),
            dma((nc, shards)),
            dma((nc, shards)),
        ],
        compiler_params=pltpu.CompilerParams(
            collective_id=0, has_side_effects=True, vmem_limit_bytes=56 * 1024 * 1024
        ),
        name="mixer",
    )(
        qkv.transpose(0, 2, 1, 3),
        fir_buffer.transpose(2, 1, 0, 3),
        fir_taps,
        finished,
        modal_state,
        poles,
        residues,
        skip[None],
        out_weight,
        norm_gain[None],
        finished,
        dest_group,
    )
    mixed, state, lagged = outs
    return (mixed, state, lagged.transpose(2, 1, 0, 3))


def solution(mesh):
    return jax.shard_map(
        per_device,
        mesh=mesh,
        in_specs=(
            P(None, "dp", None, "tensor"),
            P("dp", None, None, "tensor"),
            P(None, None, "tensor"),
            P("dp", None, "tensor"),
            P(None, "tensor"),
            P(None, "tensor"),
            P("tensor"),
            P("tensor", None),
            P("tensor"),
            P(None, "dp"),
            P(None, "dp"),
        ),
        out_specs=(P(None, "dp", "tensor"), P("dp", None, "tensor"), P("dp", None, None, "tensor")),
        check_vma=False,
    )
```

time: 97.1 us -> 77.5 us (0.80)
  Pallas kernels: 76.1 us -> 63.3 us
  other arithmetic: 11.2 us -> 0 us
  local copies, waits for them, and re-layouts: 8.68 us -> 13.2 us
    pallas_call x1, Pallas kernels: 76.1 us -> 63.3 us  [per_device(): pl.pallas_call(functools.partial(kernel, groups, shards, chunks), out_sha...]
    unnamed x16 -> x4, local copies, waits for them, and re-layouts: 3.07 us -> 13.2 us
    concatenate x2 -> x0, other arithmetic: 6.65 us -> none  [the longest x1 5.77 us: per_device(): state = jnp.concatenate(outs[nc:2 * nc], axis=0)]
    slice x9 -> x0, local copies, waits for them, and re-layouts: 2.19 us -> none  [the longest x2 1.33 us: per_device(): qkv[:, :moving].reshape(STEPS, groups, CAP, 3, chans)]
    pad x2 -> x0, other arithmetic: 1.93 us -> none  [the longest x1 1.08 us: per_device(): q_bands = jnp.pad(q_bands, ((0, 0), (0, 0), (0, 2), (0, 0)))]
    mul x1 -> x0, other arithmetic: 1.09 us -> none  [per_device(): stayed = qkv[2, moving:] * alive[2, moving:].astype(bf16)[:, None, None]]
    another operation x1 -> x0, local copies, waits for them, and re-layouts: 1.07 us -> none  [per_device(): jnp.stack([qkv[3], jnp.concatenate([moved, stayed], axis=0)], axis=2)]
where the time goes in v2:
time: 77.5 us; the launch traced here: 77.2 us
  Pallas kernels  63.3 us (82%)
  local copies, waits for them, and re-layouts  13.2 us (17%)
    pallas_call x1, Pallas kernels, per_device(): pl.pallas_call(functools.partial(kernel, groups, shards, chunks), out_sha...  63.3 us
    unnamed x4, local copies, waits for them, and re-layouts  13.2 us

profile of v2, /device:TPU:0, one launch (start us, length us, event | category | flops | bytes accessed | tf_op | source)
XLA Modules:
  0.0 77.2 jit_solution(16390199735529618531)
XLA Ops:
  0.6 2.4 %copy.17 = bf16[80,3,2,1024]{3,0,1,2:T(8,128)(2,1)} copy(bf16[80,3,2,1024]{3,2,1,0:T(2,128)(2,1)} %param.12) | data formatting | bytes 1966080 | tf_op args[1]
  3.0 63.3 %mixer.1 = (bf16[4,80,1024]{2,1,0:T(8,128)(2,1)}, f32[80,16,1024]{2,1,0:T(8,128)}, bf16[2,3,80,1024]{3,2,1,0:T(8,128)(2,1)}) custom-call(bf16[4,3,80,1024]{3,2,1,0:T(8,128)(2,1)} %bitcast.8, bf16[2,3,80,1024]{3,2,1,0:T(8,128)(2,1)} %bitcast.7, f32[3,3,1024]{2,1,0:T(4,128)} %refs_2_.1, s32[3,80]{1,0:T(4,128)} %refs_10_.1, f32[80,16,1024]{2,1,0:T(8,128)} %refs_4_.1, ...), custom_call_target="tpu_custom_call" | custom-call | tf_op jit(solution)/shard_map/mixer/pallas_call | solution.py:459
  66.3 3.2 %copy.15 = bf16[80,3,2,1024]{3,2,1,0:T(2,128)(2,1)} copy(bf16[80,3,2,1024]{3,0,1,2:T(8,128)(2,1)} %bitcast.9) | data formatting | bytes 1966080
  69.5 2.0 %copy.20 = bf16[4,80,1024]{2,1,0:T(8,128)(2,1)} copy(bf16[4,80,1024]{2,1,0:T(8,128)(2,1)} %get-tuple-element.15) | data formatting | bytes 1310720
  71.5 5.7 %copy.21 = f32[80,16,1024]{2,1,0:T(8,128)} copy(f32[80,16,1024]{2,1,0:T(8,128)} %get-tuple-element.16) | data formatting | bytes 10485760

commit v3 on v2

--- a/solution.py
+++ b/solution.py
@@ -494,7 +494,7 @@
             dma((nc, shards)),
         ],
         compiler_params=pltpu.CompilerParams(
-            collective_id=0, has_side_effects=True, vmem_limit_bytes=56 * 1024 * 1024
+            collective_id=0, has_side_effects=True, vmem_limit_bytes=38 * 1024 * 1024
         ),
         name="mixer",
     )(

time: 77.5 us -> 78 us (level)
  local copies, waits for them, and re-layouts: 13.2 us -> 15.8 us
  Pallas kernels: 63.3 us -> 61 us
    unnamed x4 -> x22, local copies, waits for them, and re-layouts: 13.2 us -> 15.8 us
    pallas_call x1, Pallas kernels: 63.3 us -> 61 us  [per_device(): pl.pallas_call(functools.partial(kernel, groups, shards, chunks), out_sha...]
where the time goes in v3:
time: 78 us; the launch traced here: 77.5 us
  Pallas kernels  61 us (78%)
  local copies, waits for them, and re-layouts  15.8 us (20%)
    pallas_call x1, Pallas kernels, per_device(): pl.pallas_call(functools.partial(kernel, groups, shards, chunks), out_sha...  61 us
    unnamed x22, local copies, waits for them, and re-layouts  15.8 us

profile of v3, /device:TPU:0, one launch (start us, length us, event | category | flops | bytes accessed | tf_op | source)
XLA Modules:
  0.0 77.5 jit_solution(2025354818554638363)
XLA Ops:
  0.6 1.5 %copy.17 = bf16[80,3,2,1024]{3,0,1,2:T(8,128)(2,1)S(1)} copy(bf16[80,3,2,1024]{3,2,1,0:T(2,128)(2,1)} %param.12) | data formatting | bytes 1966080 | tf_op args[1]
  2.1 0.0 copy-start
  2.1 2.5 %copy-done = f32[80,16,1024]{2,1,0:T(8,128)S(1)} copy-done((f32[80,16,1024]{2,1,0:T(8,128)S(1)}, f32[80,16,1024]{2,1,0:T(8,128)}, u32[]{:S(2)}) %copy-start) | copy-done | bytes 5242904
  4.6 0.0 copy-start.1
  4.6 1.5 %copy-done.1 = bf16[4,80,3,1024]{3,1,2,0:T(8,128)(2,1)S(1)} copy-done((bf16[4,80,3,1024]{3,1,2,0:T(8,128)(2,1)S(1)}, bf16[4,80,3,1024]{3,1,2,0:T(8,128)(2,1)}, u32[]{:S(2)}) %copy-start.1) | copy-done | bytes 1966104
  6.1 0.0 copy-start.2
  6.1 0.8 %copy-done.2 = f32[16,1024]{1,0:T(8,128)S(1)} copy-done((f32[16,1024]{1,0:T(8,128)S(1)}, f32[16,1024]{1,0:T(8,128)}, u32[]{:S(2)}) %copy-start.2) | copy-done | bytes 65560
  7.0 0.0 copy-start.3
  7.0 0.8 %copy-done.3 = f32[16,1024]{1,0:T(8,128)S(1)} copy-done((f32[16,1024]{1,0:T(8,128)S(1)}, f32[16,1024]{1,0:T(8,128)}, u32[]{:S(2)}) %copy-start.3) | copy-done | bytes 65560
  7.8 0.0 copy-start.4
  7.8 0.8 %copy-done.4 = f32[3,3,1024]{2,1,0:T(4,128)S(1)} copy-done((f32[3,3,1024]{2,1,0:T(4,128)S(1)}, f32[3,3,1024]{2,1,0:T(4,128)}, u32[]{:S(2)}) %copy-start.4) | copy-done | bytes 36888
  8.6 0.0 copy-start.5
  8.6 0.7 copy-done.5
  9.3 0.0 copy-start.6
  9.3 0.7 copy-done.6
  10.0 0.0 copy-start.7
  10.0 0.7 copy-done.7
  10.7 0.0 copy-start.8
  10.7 0.7 copy-done.8
  11.4 61.0 %mixer.1 = (bf16[4,80,1024]{2,1,0:T(8,128)(2,1)S(1)}, f32[80,16,1024]{2,1,0:T(8,128)S(1)}, bf16[2,3,80,1024]{3,2,1,0:T(8,128)(2,1)S(1)}) custom-call(bf16[4,3,80,1024]{3,2,1,0:T(8,128)(2,1)S(1)} %bitcast.8, bf16[2,3,80,1024]{3,2,1,0:T(8,128)(2,1)S(1)} %bitcast.7, f32[3,3,1024]{2,1,0:T(4,128)S(1)} %copy-done.4, s32[3,80]{1,0:T(4,128)S(1)} %copy-done.5, ...), custom_call_target="tpu_custom_call" | custom-call | tf_op jit(solution)/shard_map/mixer/pallas_call | solution.py:459
  72.4 2.0 %copy.15 = bf16[80,3,2,1024]{3,2,1,0:T(2,128)(2,1)} copy(bf16[80,3,2,1024]{3,0,1,2:T(8,128)(2,1)S(1)} %bitcast.9) | data formatting | bytes 1966080
  74.4 0.8 %copy.20 = bf16[4,80,1024]{2,1,0:T(8,128)(2,1)} copy(bf16[4,80,1024]{2,1,0:T(8,128)(2,1)S(1)} %get-tuple-element.15) | data formatting | bytes 1310720
  75.2 2.4 %copy.21 = f32[80,16,1024]{2,1,0:T(8,128)} copy(f32[80,16,1024]{2,1,0:T(8,128)S(1)} %get-tuple-element.16) | data formatting | bytes 10485760
Async XLA Ops:
  2.1 2.5 %copy-start = (f32[80,16,1024]{2,1,0:T(8,128)S(1)}, f32[80,16,1024]{2,1,0:T(8,128)}, u32[]{:S(2)}) copy-start(f32[80,16,1024]{2,1,0:T(8,128)} %refs_4_.1) | copy-start | bytes 15728644
  4.6 1.5 %copy-start.1 = (bf16[4,80,3,1024]{3,1,2,0:T(8,128)(2,1)S(1)}, bf16[4,80,3,1024]{3,1,2,0:T(8,128)(2,1)}, u32[]{:S(2)}) copy-start(bf16[4,80,3,1024]{3,1,2,0:T(8,128)(2,1)} %param.11) | copy-start | bytes 5898244
  6.1 0.8 %copy-start.2 = (f32[16,1024]{1,0:T(8,128)S(1)}, f32[16,1024]{1,0:T(8,128)}, u32[]{:S(2)}) copy-start(f32[16,1024]{1,0:T(8,128)} %refs_5_.1) | copy-start | bytes 196612
  7.0 0.8 %copy-start.3 = (f32[16,1024]{1,0:T(8,128)S(1)}, f32[16,1024]{1,0:T(8,128)}, u32[]{:S(2)}) copy-start(f32[16,1024]{1,0:T(8,128)} %refs_6_.1) | copy-start | bytes 196612
  7.8 0.8 %copy-start.4 = (f32[3,3,1024]{2,1,0:T(4,128)S(1)}, f32[3,3,1024]{2,1,0:T(4,128)}, u32[]{:S(2)}) copy-start(f32[3,3,1024]{2,1,0:T(4,128)} %refs_2_.1) | copy-start | bytes 110596
  8.6 0.7 copy-start.5
  9.3 0.7 copy-start.6
  10.0 0.7 copy-start.7
  10.7 0.7 copy-start.8

commit v4 on v3

--- a/solution.py
+++ b/solution.py
@@ -28,15 +28,18 @@
         return got
 
     nc = len(chunks)
-    q_ref, l_ref, tap_ref, fin_ref = take(4)
-    st_ref, pole_ref, res_ref, skip_ref, w_hbm, gain_ref = take(6)
+    l_ref, fin_ref, st_ref, w_hbm = take(4)
+    small_hbm = take(6)
     done_ref, dest_ref = take(2)
     mix_out, st_out, lag_out = take(3)
     s_refs = take(nc)
+    small_refs = take(6)
+    q_ref, tap_ref, pole_ref, res_ref, skip_ref, gain_ref = small_refs
     w_ref, lagn, lagm, msend = take(4)
     mrecv = take(STEPS - 1)
     xm, pm, ym, xs, ps, ys = take(6)
-    g_refs, p_refs, r_refs, relay_refs, t_refs = take(nc), take(nc), take(nc), take(nc), take(nc)
+    np = nc + 1
+    g_refs, p_refs, r_refs, relay_refs, t_refs = take(np), take(np), take(np), take(np), take(np)
     ss_own, ss_recv = take(2)
     load_sem, store_sem, ms_sem, mr_sem, rs_sem, rr_sem, rl_sem, ss_sem, sr_sem = take(9)
     sm = s_refs[0]
@@ -68,6 +71,11 @@
         pltpu.make_async_copy(s_refs[c], st_out.at[pl.ds(firsts[c], chunks[c])], store_sem.at[c])
         for c in range(nc)
     ]
+    small_loads = [
+        pltpu.make_async_copy(small_hbm[i], small_refs[i], load_sem.at[nc + 1 + i]) for i in range(6)
+    ]
+    for load in small_loads:
+        load.start()
     loads[0].start()
     loads[1].start()
     load_w.start()
@@ -168,7 +176,8 @@
                             lagm[i * (8 // CAP) + u, at : at + CAP, :] = lag[u * CAP : u * CAP + CAP]
 
     def moving_gate(turn):
-        g_refs[0][turn * chunks[0] : (turn + 1) * chunks[0], :] = (
+        g_ref, at = (g_refs[nc], turn * chunks[0]) if turn < STEPS - 1 else (g_refs[0], 0)
+        g_ref[at : at + chunks[0], :] = (
             xm[...] * (ym[...] + skip_ref[...] * pm[...])
         ).astype(jnp.bfloat16)
 
@@ -355,7 +364,8 @@
             square_copy(c, j).start()
 
     def finish(c):
-        t_ref, rows, first = t_refs[c], chunks[c], firsts[c]
+        t_ref, rows, first = t_refs[c], chunks[c % nc], firsts[c % nc]
+        turn_at = STEPS - 1 if c == 0 else 0
         for j in range(1, shards):
             square_copy(c, j).wait_recv()
         total = ss_own[c]
@@ -367,7 +377,7 @@
             value = (t_ref[i : i + size, :] * scale * gain_ref[...]).astype(jnp.bfloat16)
             for turn in range(i // rows, (i + size) // rows):
                 part = turn * rows - i
-                mix_out[turn, first : first + rows, :] = value[part : part + rows]
+                mix_out[turn_at + turn, first : first + rows, :] = value[part : part + rows]
 
     def stay(c):
         loads[c].wait()
@@ -377,6 +387,8 @@
             load_w.wait()
         project(c)
 
+    for load in small_loads:
+        load.wait()
     loads[0].wait()
     moving_step(0)
     pl.semaphore_wait(barrier, groups + shards - 2)
@@ -394,6 +406,7 @@
     moving_step(2)
     send_moving(2)
     moving_gate(2)
+    project(nc)
     for c in range(2, nc):
         relay(c)
     await_moving(2)
@@ -401,11 +414,12 @@
     moving_gate(3)
     stores[0].start()
     project(0)
+    relay(nc)
     collect(1)
     relay(0)
-    for c in range(2, nc):
+    for c in range(2, nc + 1):
         collect(c)
-    for c in range(1, nc):
+    for c in range(1, nc + 1):
         finish(c)
     collect(0)
     finish(0)
@@ -413,7 +427,7 @@
         @pl.loop(1, groups)
         def _(d):
             migration(turn, d).wait_send()
-    for c in range(nc):
+    for c in range(nc + 1):
         @pl.loop(0, shards)
         def _(s):
             @pl.when(s != z)
@@ -451,11 +465,18 @@
     half = left // 32 * 16
     chunks = (moving,) + ((half, left - half) if half else (left,))
     nc = len(chunks)
-    tall = [STEPS * n for n in chunks]
+    tall = [moving] + [STEPS * n for n in chunks[1:]] + [(STEPS - 1) * moving]
     vmem = pl.BlockSpec(memory_space=pltpu.VMEM)
     smem = pl.BlockSpec(memory_space=pltpu.SMEM)
-    hbm = pl.BlockSpec(memory_space=pl.ANY)
+    anywhere = pl.BlockSpec(memory_space=pl.ANY)
+    hbm = pl.BlockSpec(memory_space=pltpu.HBM)
     dma = pltpu.SemaphoreType.DMA
+    small = (qkv.transpose(0, 2, 1, 3), fir_taps, poles, residues, skip[None], norm_gain[None])
+    pin = functools.partial(pltpu.with_memory_space_constraint, memory_space=pltpu.HBM)
+    small = tuple(pin(x) for x in small)
+    modal_state, out_weight, finished, dest_group = map(
+        pin, (modal_state, out_weight, finished, dest_group)
+    )
     outs = pl.pallas_call(
         functools.partial(kernel, groups, shards, chunks),
         out_shape=[
@@ -463,9 +484,10 @@
             jax.ShapeDtypeStruct(modal_state.shape, f32),
             jax.ShapeDtypeStruct((2, 3, rows, chans), bf16),
         ],
-        in_specs=[vmem] * 4 + [hbm, vmem, vmem, vmem, hbm, vmem, smem, smem],
-        out_specs=[vmem, hbm, vmem],
+        in_specs=[vmem] * 2 + [hbm] * 8 + [smem] * 2,
+        out_specs=[vmem, anywhere, vmem],
         scratch_shapes=[pltpu.VMEM((n, order, chans), f32) for n in chunks]
+        + [pltpu.VMEM(x.shape, x.dtype) for x in small]
         + [
             pltpu.VMEM(out_weight.shape, bf16),
             pltpu.VMEM((2, 3, moving, chans), f32),
@@ -481,33 +503,28 @@
         + [pltpu.VMEM((shards, n, cols), bf16) for n in tall]
         + [pltpu.VMEM((n, cols), f32) for n in tall]
         + [
-            pltpu.VMEM((nc, 8, 128), f32),
-            pltpu.VMEM((nc, shards, 8, 128), f32),
-            dma((nc + 1,)),
+            pltpu.VMEM((nc + 1, 8, 128), f32),
+            pltpu.VMEM((nc + 1, shards, 8, 128), f32),
+            dma((nc + 7,)),
             dma((nc,)),
             dma((STEPS - 1, groups)),
             dma((STEPS - 1, groups)),
-            dma((nc, shards)),
-            dma((nc, 4)),
-            dma((nc, shards)),
-            dma((nc, shards)),
-            dma((nc, shards)),
+            dma((nc + 1, shards)),
+            dma((nc + 1, 4)),
+            dma((nc + 1, shards)),
+            dma((nc + 1, shards)),
+            dma((nc + 1, shards)),
         ],
         compiler_params=pltpu.CompilerParams(
             collective_id=0, has_side_effects=True, vmem_limit_bytes=38 * 1024 * 1024
         ),
         name="mixer",
     )(
-        qkv.transpose(0, 2, 1, 3),
         fir_buffer.transpose(2, 1, 0, 3),
-        fir_taps,
         finished,
         modal_state,
-        poles,
-        residues,
-        skip[None],
         out_weight,
-        norm_gain[None],
+        *small,
         finished,
         dest_group,
     )

time: 78 us -> 71.9 us (0.922)
  local copies, waits for them, and re-layouts: 15.8 us -> 6.61 us
  Pallas kernels: 61 us -> 64.5 us
    unnamed x22 -> x4, local copies, waits for them, and re-layouts: 15.8 us -> 6.61 us
    pallas_call x1, Pallas kernels: 61 us -> 64.5 us  [per_device(): pl.pallas_call(functools.partial(kernel, groups, shards, chunks), out_sha...]
where the time goes in v4:
time: 71.9 us; the launch traced here: 71.7 us
  Pallas kernels  64.5 us (90%)
  local copies, waits for them, and re-layouts  6.61 us (9%)
    pallas_call x1, Pallas kernels, per_device(): pl.pallas_call(functools.partial(kernel, groups, shards, chunks), out_sha...  64.5 us
    unnamed x4, local copies, waits for them, and re-layouts  6.61 us

profile of v4, /device:TPU:0, one launch (start us, length us, event | category | flops | bytes accessed | tf_op | source)
XLA Modules:
  0.0 71.7 jit_solution(2842713685126661365)
XLA Ops:
  0.6 1.5 %copy.17 = bf16[80,3,2,1024]{3,0,1,2:T(8,128)(2,1)S(1)} copy(bf16[80,3,2,1024]{3,2,1,0:T(2,128)(2,1)} %param.12) | data formatting | bytes 1966080 | tf_op args[1]
  2.1 64.5 %mixer.1 = (bf16[4,80,1024]{2,1,0:T(8,128)(2,1)S(1)}, f32[80,16,1024]{2,1,0:T(8,128)S(1)}, bf16[2,3,80,1024]{3,2,1,0:T(8,128)(2,1)S(1)}) custom-call(bf16[2,3,80,1024]{3,2,1,0:T(8,128)(2,1)S(1)} %bitcast.7, s32[3,80]{1,0:T(4,128)} %refs_10_.1, f32[80,16,1024]{2,1,0:T(8,128)} %refs_2_.1, bf16[1024,4096]{1,0:T(8,128)(2,1)} %refs_3_.1, ...), custom_call_target="tpu_custom_call" | custom-call | tf_op jit(solution)/shard_map/mixer/pallas_call | solution.py:480
  66.6 2.0 %copy.15 = bf16[80,3,2,1024]{3,2,1,0:T(2,128)(2,1)} copy(bf16[80,3,2,1024]{3,0,1,2:T(8,128)(2,1)S(1)} %bitcast.8) | data formatting | bytes 1966080
  68.5 0.8 %copy.20 = bf16[4,80,1024]{2,1,0:T(8,128)(2,1)} copy(bf16[4,80,1024]{2,1,0:T(8,128)(2,1)S(1)} %get-tuple-element.15) | data formatting | bytes 1310720
  69.4 2.4 %copy.21 = f32[80,16,1024]{2,1,0:T(8,128)} copy(f32[80,16,1024]{2,1,0:T(8,128)S(1)} %get-tuple-element.16) | data formatting | bytes 10485760

commit v5 on v4

--- a/solution.py
+++ b/solution.py
@@ -76,9 +76,9 @@
     ]
     for load in small_loads:
         load.start()
-    loads[0].start()
     loads[1].start()
     load_w.start()
+    loads[0].start()
     for load in loads[2:]:
         load.start()
     ss_own[...] = jnp.zeros_like(ss_own)
@@ -321,8 +321,9 @@
 
     here = [z >= 1, z >= 2, z <= shards - 2, z <= shards - 3]
 
-    def pieces(rows):
-        return [(i, min(128, rows - i)) for i in range(0, rows, 128)]
+    def pieces(c):
+        rows, step = t_refs[c].shape[0], 128 // chunks[c % nc] * chunks[c % nc]
+        return [(i, min(step, rows - i)) for i in range(0, rows, step)]
 
     def eye(size):
         return lax.broadcasted_iota(jnp.int32, (size, 128), 0) == lax.broadcasted_iota(
@@ -354,7 +355,7 @@
                 ).wait_recv()
                 t_ref[...] += r_ref[slot].astype(jnp.float32)
 
-        for at, (i, size) in enumerate(pieces(t_ref.shape[0])):
+        for at, (i, size) in enumerate(pieces(c)):
             x = t_ref[i : i + size, :]
             squares = jnp.sum(x * x, axis=1, keepdims=True)
             ss_own[c, at : at + 1, :] = jnp.sum(
@@ -371,7 +372,7 @@
         total = ss_own[c]
         for j in range(1, shards):
             total = total + ss_recv[c, j]
-        for at, (i, size) in enumerate(pieces(t_ref.shape[0])):
+        for at, (i, size) in enumerate(pieces(c)):
             squares = jnp.sum(jnp.where(eye(size), total[at : at + 1], 0.0), axis=1, keepdims=True)
             scale = lax.rsqrt(squares / (cols * shards) + 1e-05)
             value = (t_ref[i : i + size, :] * scale * gain_ref[...]).astype(jnp.bfloat16)
@@ -385,23 +386,23 @@
         stores[c].start()
         if c == 1:
             load_w.wait()
+            pl.semaphore_wait(barrier, groups + shards - 2)
         project(c)
 
     for load in small_loads:
         load.wait()
+    stay(1)
     loads[0].wait()
     moving_step(0)
-    pl.semaphore_wait(barrier, groups + shards - 2)
     send_moving(0)
     moving_gate(0)
-    stay(1)
+    for c in range(2, nc):
+        stay(c)
     await_moving(0)
     moving_step(1)
     send_moving(1)
     moving_gate(1)
     relay(1)
-    for c in range(2, nc):
-        stay(c)
     await_moving(1)
     moving_step(2)
     send_moving(2)
@@ -462,7 +463,7 @@
 
     moving = groups * CAP
     left = rows - moving
-    half = left // 32 * 16
+    half = 16 if left > 16 else 0
     chunks = (moving,) + ((half, left - half) if half else (left,))
     nc = len(chunks)
     tall = [moving] + [STEPS * n for n in chunks[1:]] + [(STEPS - 1) * moving]

time: 71.9 us -> 72.3 us (level)
  no operation moved by 1% of the time
where the time goes in v5:
time: 72.3 us; the launch traced here: 72.1 us
  Pallas kernels  64.9 us (90%)
  local copies, waits for them, and re-layouts  6.61 us (9%)
    pallas_call x1, Pallas kernels, per_device(): pl.pallas_call(functools.partial(kernel, groups, shards, chunks), out_sha...  64.9 us
    unnamed x4, local copies, waits for them, and re-layouts  6.61 us

profile of v5, /device:TPU:0, one launch (start us, length us, event | category | flops | bytes accessed | tf_op | source)
XLA Modules:
  0.0 72.1 jit_solution(8827905460988217970)
XLA Ops:
  0.6 1.5 %copy.17 = bf16[80,3,2,1024]{3,0,1,2:T(8,128)(2,1)S(1)} copy(bf16[80,3,2,1024]{3,2,1,0:T(2,128)(2,1)} %param.12) | data formatting | bytes 1966080 | tf_op args[1]
  2.1 64.9 %mixer.1 = (bf16[4,80,1024]{2,1,0:T(8,128)(2,1)S(1)}, f32[80,16,1024]{2,1,0:T(8,128)S(1)}, bf16[2,3,80,1024]{3,2,1,0:T(8,128)(2,1)S(1)}) custom-call(bf16[2,3,80,1024]{3,2,1,0:T(8,128)(2,1)S(1)} %bitcast.7, s32[3,80]{1,0:T(4,128)} %refs_10_.1, f32[80,16,1024]{2,1,0:T(8,128)} %refs_2_.1, bf16[1024,4096]{1,0:T(8,128)(2,1)} %refs_3_.1, ...), custom_call_target="tpu_custom_call" | custom-call | tf_op jit(solution)/shard_map/mixer/pallas_call | solution.py:481
  67.0 2.0 %copy.15 = bf16[80,3,2,1024]{3,2,1,0:T(2,128)(2,1)} copy(bf16[80,3,2,1024]{3,0,1,2:T(8,128)(2,1)S(1)} %bitcast.8) | data formatting | bytes 1966080
  68.9 0.8 %copy.20 = bf16[4,80,1024]{2,1,0:T(8,128)(2,1)} copy(bf16[4,80,1024]{2,1,0:T(8,128)(2,1)S(1)} %get-tuple-element.15) | data formatting | bytes 1310720
  69.8 2.4 %copy.21 = f32[80,16,1024]{2,1,0:T(8,128)} copy(f32[80,16,1024]{2,1,0:T(8,128)S(1)} %get-tuple-element.16) | data formatting | bytes 10485760
